TPU v7x, 512 devices: a whole 4x4x16 slice. The times are simulated.
512 devices in a mesh: dp: 16 (over x, z_hi, core), tm: 8 (over z_lo), height: 4 (over y).
Axes of the slice: x: 4, y: 4, z: 16 (z_hi: 2, z_lo: 8; z = z_hi * 8 + z_lo), core: 2. Of those that a mesh axis runs over, the one named last changes fastest.
Arguments:
- latent: bfloat16 [256, 8, 16, 512], P(('dp', 'tm'), None, None, 'height'), parts along dimension 0, may hold values from -6 to 6
- gain_latent: float32 [512], P('height'), may hold values from 0.25 to 1.75
- shift_latent: float32 [512], P('height'), may hold values from -3 to 3
- conv_latent: bfloat16 [13824, 512], P('tm', 'height'), may hold values from -0.0546875 to 0.0546875
- up_weight: bfloat16 [512, 2048], P('height'), may hold values from -0.25 to 0.25
- gain_block: float32 [256], replicated, may hold values from 0.25 to 1.75
- shift_block: float32 [256], replicated, may hold values from -3 to 3
- conv_block: bfloat16 [6912, 256], P(('tm', 'height')), may hold values from -0.078125 to 0.078125
- cotangent: bfloat16 [512, 16, 32, 256], P(('dp', 'tm'), 'height'), parts along dimension 0, may hold values from -6 to 6
Outputs:
- decoded: bfloat16 [512, 16, 32, 256], P(('dp', 'tm'), 'height'), parts along dimension 0
- grad_upsampled: bfloat16 [512, 16, 32, 256], P(('dp', 'tm'), 'height'), parts along dimension 0
- grad_weight: float32 [36864, 256], P(('dp', 'tm', 'height')), parts along dimension 0
- grad_gain: float32 [4096], P('dp'), parts along dimension 0
- grad_shift: float32 [4096], P('dp'), parts along dimension 0
There are 16 independent parts, one for each index of `dp`. A program takes and returns all parts, laid end to end along the dimension named above; an argument that names none is the same for every part. Nothing has to cross between parts.
All inputs are finite; a program needn't handle non-finite values.
Results may differ from a plain program's by a relative error of at most 0.009.
Values may be sent and summed in bfloat16 or wider, within the bound.
No kernel may reach another device: no remote copies, remote signals or barrier semaphores. Data moves between devices by JAX's collectives and lax.ppermute only.
A program may use at most 128 MiB of HBM per device.

v0:
```python
import jax
import jax.numpy as jnp
from jax import lax
from jax.sharding import PartitionSpec as P

C1 = 512
GROUPS = 32
epsilon = 1e-06


def copy_for_each(array, axis):
    devices = lax.axis_size(axis)
    return lax.all_to_all(
        jnp.broadcast_to(array[None], (devices, *array.shape)), axis, 0, 0, tiled=True
    )


def taken_together(array, axis):
    everything = copy_for_each(array, axis)
    return jnp.sum(everything, axis=0)


def packed_total(arrays, axis):
    ends = [0]
    for a in arrays:
        ends.append(ends[-1] + a.size)
    so_far = taken_together(jnp.concatenate([a.ravel() for a in arrays]), axis)
    return tuple((so_far[b:e].reshape(a.shape) for a, b, e in zip(arrays, ends, ends[1:])))


def shifted(block, axis, distance):
    devices = range(lax.axis_size(axis))
    route = [(i - distance, i) for i in devices if i - distance in devices]
    return lax.ppermute(block, axis, route)


def in_order(tiles, dim):
    tiles = jnp.moveaxis(tiles, 0, dim)
    shape = tiles.shape
    return tiles.reshape(*shape[:dim], shape[dim] * shape[dim + 1], *shape[dim + 2 :])


def gather_directly(array, axis, dim):
    tiles = copy_for_each(array, axis)
    return in_order(tiles, dim)


def extended_2(cells, sides, width):
    for axis, dim in sides:
        count = lax.axis_size(axis)
        ends = count - 1
        head = lax.slice_in_dim(cells, 0, width, axis=dim)
        tail = lax.slice_in_dim(cells, cells.shape[dim] - width, cells.shape[dim], axis=dim)
        cells = jnp.concatenate(
            [
                lax.ppermute(tail, axis, [(i, (i + 1) % count) for i in range(ends)]),
                cells,
                lax.ppermute(head, axis, [((i + 1) % count, i) for i in range(ends)]),
            ],
            axis=dim,
        )
    return cells


def gather_in_order(array, axes, turns):
    tiles = array
    for k in turns:
        tiles = lax.all_gather(tiles, axes[k])
    done = turns[::-1]
    back = [done.index(k) for k in range(len(axes))]
    tiles = tiles.transpose(*back, *range(len(axes), tiles.ndim))
    return tiles.reshape(-1, *array.shape)


def whole_of(array, axes, turns, dim):
    return in_order(gather_in_order(array, axes, turns), dim)


def cut_along(array, dim, devices):
    before, after = (array.shape[:dim], array.shape[dim + 1 :])
    return jnp.moveaxis(array.reshape(*before, devices, -1, *after), dim, 0)


def sum_at_owner(array, axis, dim):
    tiles = cut_along(array, dim, lax.axis_size(axis))
    arrived = lax.all_to_all(tiles, axis, split_axis=0, concat_axis=0, tiled=True)
    return arrived.sum(axis=0)


def standardize(values, mean_value, inverse, groups):
    shape_full = values.shape
    grouped = values.reshape(shape_full[:-1] + (groups, shape_full[-1] // groups))
    return ((grouped - mean_value[:, None]) * inverse[:, None]).reshape(shape_full)


def causal_taps(padded, weight, frames, rows, cols):
    channels_in = padded.shape[-1]
    summed = jnp.zeros((frames * rows * cols, weight.shape[1]), jnp.float32)
    for lag_step in range(3):
        for row_step in range(3):
            for col_step in range(3):
                tap_index = (lag_step * 3 + row_step) * 3 + col_step
                window = padded[
                    lag_step : lag_step + frames,
                    row_step : row_step + rows,
                    col_step : col_step + cols,
                ]
                kernel = weight[tap_index * channels_in : (tap_index + 1) * channels_in]
                summed = summed + jnp.dot(
                    window.reshape(-1, channels_in), kernel, preferred_element_type=jnp.float32
                )
    return summed.reshape(frames, rows, cols, weight.shape[1])


def transposed_taps(padded, weight, frames, rows, cols):
    channels_out = padded.shape[-1]
    channels_in = weight.shape[0] // 27
    summed = jnp.zeros((frames * rows * cols, channels_in), jnp.float32)
    for lag_step in range(3):
        for row_step in range(3):
            for col_step in range(3):
                tap_index = (lag_step * 3 + row_step) * 3 + col_step
                window = padded[
                    2 - lag_step : 2 - lag_step + frames,
                    2 - row_step : 2 - row_step + rows,
                    2 - col_step : 2 - col_step + cols,
                ]
                kernel = weight[tap_index * channels_in : (tap_index + 1) * channels_in]
                summed = summed + lax.dot_general(
                    window.reshape(-1, channels_out),
                    kernel,
                    (((1,), (1,)), ((), ())),
                    preferred_element_type=jnp.float32,
                )
    return summed.reshape(frames, rows, cols, channels_in)


def weight_terms(padded, grads, frames, rows, cols):
    channels_in = padded.shape[-1]
    flat_grads = grads.reshape(-1, grads.shape[-1])
    blocks = []
    for row_step in range(3):
        for col_step in range(3):
            window = padded[2 : 2 + frames, row_step : row_step + rows, col_step : col_step + cols]
            blocks.append(
                lax.dot_general(
                    window.reshape(-1, channels_in),
                    flat_grads,
                    (((0,), (0,)), ((), ())),
                    preferred_element_type=jnp.float32,
                )
            )
    return jnp.concatenate(blocks, 0)


def local(
    latent,
    gain_latent,
    shift_latent,
    conv_latent,
    up_weight,
    gain_block,
    shift_block,
    conv_block,
    cotangent,
):
    per_group = C1 // GROUPS
    groups_here = latent.shape[-1] // per_group
    latent_f32 = latent.astype(jnp.float32)
    grouped = latent_f32.reshape(-1, groups_here, per_group)
    first_sums = jnp.sum(grouped, axis=(0, 2))
    second_sums = jnp.sum(grouped * grouped, axis=(0, 2))
    first_totals, second_totals = packed_total((first_sums, second_sums), "tm")
    count_latent = grouped.shape[0] * per_group * lax.axis_size("tm")
    mean_latent = first_totals / count_latent
    inverse_latent = lax.rsqrt(second_totals / count_latent - mean_latent * mean_latent + epsilon)
    normed = (
        standardize(latent_f32, mean_latent, inverse_latent, groups_here) * gain_latent
        + shift_latent
    )
    active = jax.nn.silu(normed).astype(jnp.bfloat16)
    earlier = shifted(active, "tm", 1)
    extended = jnp.concatenate([earlier, active], 0)
    all_channels = gather_directly(extended, "height", 3)
    padded = jnp.pad(all_channels, ((0, 0), (1, 1), (1, 1), (0, 0)))
    latent_weight = lax.all_gather(conv_latent, "tm", axis=0, tiled=True)
    frames_latent, rows_latent, cols_latent = (latent.shape[0], latent.shape[1], latent.shape[2])
    mixed = causal_taps(padded, latent_weight, frames_latent, rows_latent, cols_latent)
    refined = (latent_f32 + mixed).astype(jnp.bfloat16)
    band_rows = rows_latent // lax.axis_size("height")
    own_band = lax.all_to_all(refined, "height", split_axis=1, concat_axis=3, tiled=True)
    flat_band = own_band.reshape(-1, own_band.shape[-1])
    expanded = jnp.dot(
        flat_band, gather_directly(up_weight, "height", 0), preferred_element_type=jnp.float32
    )
    channels_block = up_weight.shape[1] // 8
    spread = expanded.reshape(frames_latent, band_rows, cols_latent, 2, 2, 2, channels_block)
    spread = spread.transpose(0, 3, 1, 4, 2, 5, 6)
    upsampled = spread.reshape(
        2 * frames_latent, 2 * band_rows, 2 * cols_latent, channels_block
    ).astype(jnp.bfloat16)
    frames_block, rows_block, cols_block = (
        upsampled.shape[0],
        upsampled.shape[1],
        upsampled.shape[2],
    )
    up_f32 = upsampled.astype(jnp.float32)
    per_block = channels_block // GROUPS
    grouped_block = up_f32.reshape(-1, GROUPS, per_block)
    block_first = jnp.sum(grouped_block, axis=(0, 2))
    block_second = jnp.sum(grouped_block * grouped_block, axis=(0, 2))
    block_first, block_second = packed_total((block_first, block_second), ("tm", "height"))
    count_block = grouped_block.shape[0] * per_block * lax.axis_size("tm") * lax.axis_size("height")
    mean_block = block_first / count_block
    inverse_block = lax.rsqrt(block_second / count_block - mean_block * mean_block + epsilon)
    standard = standardize(up_f32, mean_block, inverse_block, GROUPS)
    normed_block = standard * gain_block + shift_block
    active_block = jax.nn.silu(normed_block).astype(jnp.bfloat16)
    before = shifted(active_block[-2:], "tm", 1)
    ext_block = jnp.concatenate([before, active_block], 0)
    beside_all = extended_2(ext_block, (("height", 1),), 1)
    padded_block = jnp.pad(beside_all, ((0, 0), (0, 0), (1, 1), (0, 0)))
    block_weight = whole_of(conv_block, ("tm", "height"), (0, 1), 0)
    mixed_block = causal_taps(padded_block, block_weight, frames_block, rows_block, cols_block)
    decoded = (up_f32 + mixed_block).astype(jnp.bfloat16)
    after = shifted(cotangent[:2], "tm", -1)
    grad_ext = jnp.concatenate([cotangent, after], 0)
    grad_around = extended_2(grad_ext, (("height", 1),), 1)
    grad_padded = jnp.pad(grad_around, ((0, 0), (0, 0), (1, 1), (0, 0)))
    grad_active = transposed_taps(grad_padded, block_weight, frames_block, rows_block, cols_block)
    local_terms = weight_terms(padded_block, cotangent, frames_block, rows_block, cols_block)
    time_summed = sum_at_owner(local_terms, "tm", 0)
    grad_weight = sum_at_owner(time_summed, "height", 0)
    sigmoid = jax.nn.sigmoid(normed_block)
    grad_normed = grad_active * sigmoid * (1.0 + normed_block * (1.0 - sigmoid))
    flat_grad = grad_normed.reshape(-1, channels_block)
    flat_standard = standard.reshape(-1, channels_block)
    grad_shift, grad_gain = packed_total(
        (jnp.sum(flat_grad, axis=0), jnp.sum(flat_grad * flat_standard, axis=0)), ("tm", "height")
    )
    first_mean = jnp.sum((gain_block * grad_shift).reshape(GROUPS, per_block), axis=1) / count_block
    second_mean = jnp.sum((gain_block * grad_gain).reshape(GROUPS, per_block), axis=1) / count_block
    grouped_grad = (grad_normed * gain_block).reshape(-1, GROUPS, per_block)
    grouped_standard = standard.reshape(-1, GROUPS, per_block)
    corrected = (
        grouped_grad - first_mean[:, None] - grouped_standard * second_mean[:, None]
    ) * inverse_block[:, None]
    grad_upsampled = (cotangent.astype(jnp.float32) + corrected.reshape(cotangent.shape)).astype(
        jnp.bfloat16
    )
    return (decoded, grad_upsampled, grad_weight, grad_gain, grad_shift)


def solution(mesh):
    return jax.shard_map(
        local,
        mesh=mesh,
        in_specs=(
            P(("dp", "tm"), None, None, "height"),
            P("height"),
            P("height"),
            P("tm", "height"),
            P("height", None),
            P(),
            P(),
            P(("tm", "height"), None),
            P(("dp", "tm"), "height", None, None),
        ),
        out_specs=(
            P(("dp", "tm"), "height", None, None),
            P(("dp", "tm"), "height", None, None),
            P(("dp", "tm", "height"), None),
            P("dp"),
            P("dp"),
        ),
        check_vma=False,
    )
```

profile of v0, /device:TPU:2, one launch (start us, length us, event | category | flops | bytes accessed | tf_op | source)
XLA Modules:
  0.0 456.5 jit_solution(3244054950084139941)
XLA Ops:
  7.2 54.2 %all-gather = bf16[1728,256]{1,0:T(8,128)(2,1)} all-gather(bf16[216,256]{1,0:T(8,128)(2,1)} %param.16), channel_id=2, replica_groups=mesh['dp'=16,'tm'=8,'height'=4] {'tm'}, dimensions={0}, use_global_device_ids=true | all-gather | bytes 995328 | tf_op jit(solution)/shard_map/all_gather | solution.py:68
  63.4 10.3 %all-to-all-start = ((f32[8,1,16]{2,1,0:T(1,128)}), f32[8,1,16]{2,1,0:T(1,128)S(1)}, u32[]{:S(2)}, u32[]{:S(2)}) async-start(f32[8,1,16]{2,1,0:T(1,128)} %broadcast_in_dim.10), calls=%async_computation | async-start | bytes 8192 | tf_op jit(solution)/shard_map/all_to_all | solution.py:13
  75.9 8.1 %all-to-all-done = f32[8,1,16]{2,1,0:T(1,128)S(1)} async-done(((f32[8,1,16]{2,1,0:T(1,128)}), f32[8,1,16]{2,1,0:T(1,128)S(1)}, u32[]{:S(2)}, u32[]{:S(2)}) %all-to-all-start) | async-done | bytes 544 | tf_op jit(solution)/shard_map/all_to_all | solution.py:13
  85.3 2.5 collective-permute-start
  90.7 4.5 all-to-all-start.1
  96.5 4.6 collective-permute-start.5
  101.4 8.3 %all-to-all-done.1 = bf16[4,4,8,16,128]{4,3,2,1,0:T(8,128)(2,1)S(1)} async-done(((bf16[4,4,8,16,128]{4,3,2,1,0:T(8,128)(2,1)}), bf16[4,4,8,16,128]{4,3,2,1,0:T(8,128)(2,1)S(1)}, u32[]{:S(2)}, u32[]{:S(2)}) %all-to-all-start.1) | async-done | bytes 524320 | tf_op jit(solution)/shard_map/all_to_all | solution.py:13
  111.3 3.6 all-to-all-start.3
  123.1 2.4 pad_slice_fusion
  125.4 19.1 %all-to-all-done.3 = bf16[4,128,2048]{1,2,0:T(8,128)(2,1)S(1)} async-done(((bf16[4,128,2048]{1,2,0:T(8,128)(2,1)}), bf16[4,128,2048]{1,2,0:T(8,128)(2,1)S(1)}, u32[]{:S(2)}, u32[]{:S(2)}) %all-to-all-start.3) | async-done | bytes 2097184 | tf_op jit(solution)/shard_map/all_to_all | solution.py:13
  144.5 2.6 copy.75
  147.2 3.9 copy.76
  151.1 2.4 copy.79
  161.2 68.7 %all-gather.5.cloned.1.call-done = bf16[13824,128]{1,0:T(8,128)(2,1)} async-done(((bf16[1728,128]{1,0:T(8,128)(2,1)}), bf16[13824,128]{1,0:T(8,128)(2,1)}) %all-gather.5.cloned.1.call-update) | async-done | bytes 3538960 | tf_op jit(solution)/shard_map/all_gather | solution.py:186
  245.2 4.2 all-to-all-start.2
  251.6 3.6 all-to-all-done.2
  258.2 3.7 fusion.146
  266.1 4.8 %all-to-all-start.4 = ((f32[32,1,64]{2,1,0:T(1,128)}), f32[32,1,64]{2,1,0:T(1,128)S(1)}, u32[]{:S(2)}, u32[]{:S(2)}) async-start(f32[32,1,64]{2,1,0:T(1,128)} %broadcast_in_dim.13), calls=%async_computation.4 | async-start | bytes 32768 | tf_op jit(solution)/shard_map/all_to_all | solution.py:13
  272.9 2.2 copy.77
  275.2 2.2 reshape.485
  277.4 5.9 %all-to-all-done.4 = f32[32,1,64]{2,1,0:T(1,128)S(1)} async-done(((f32[32,1,64]{2,1,0:T(1,128)}), f32[32,1,64]{2,1,0:T(1,128)S(1)}, u32[]{:S(2)}, u32[]{:S(2)}) %all-to-all-start.4) | async-done | bytes 8224 | tf_op jit(solution)/shard_map/all_to_all | solution.py:13
  287.1 2.8 fusion.145
  290.6 6.5 %all-to-all-start.5 = ((f32[32,1,512]{2,1,0:T(1,128)}), f32[32,1,512]{2,1,0:T(1,128)S(1)}, u32[]{:S(2)}, u32[]{:S(2)}) async-start(f32[32,1,512]{2,1,0:T(1,128)} %broadcast_in_dim.14), calls=%async_computation.5 | async-start | bytes 131072 | tf_op jit(solution)/shard_map/all_to_all | solution.py:13
  298.5 11.5 %all-to-all-done.5 = f32[32,1,512]{2,1,0:T(1,128)S(1)} async-done(((f32[32,1,512]{2,1,0:T(1,128)}), f32[32,1,512]{2,1,0:T(1,128)S(1)}, u32[]{:S(2)}, u32[]{:S(2)}) %all-to-all-start.5) | async-done | bytes 65568 | tf_op jit(solution)/shard_map/all_to_all | solution.py:13
  311.4 2.2 add_convert_fusion
  313.6 2.3 collective-permute-start.1
  315.9 2.5 collective-permute-done.1
  319.8 4.6 collective-permute-start.2
  330.8 5.2 %all-to-all-start.6 = ((f32[8,288,256]{2,1,0:T(8,128)}), f32[8,288,256]{2,1,0:T(8,128)S(1)}, u32[]{:S(2)}, u32[]{:S(2)}) async-start(f32[8,288,256]{2,1,0:T(8,128)} %bitcast.329), calls=%async_computation.6 | async-start | bytes 4718592 | tf_op jit(solution)/shard_map/all_to_all | solution.py:86
  345.7 91.6 %all-to-all-done.6 = f32[8,288,256]{2,1,0:T(8,128)S(1)} async-done(((f32[8,288,256]{2,1,0:T(8,128)}), f32[8,288,256]{2,1,0:T(8,128)S(1)}, u32[]{:S(2)}, u32[]{:S(2)}) %all-to-all-start.6) | async-done | bytes 2359328 | tf_op jit(solution)/shard_map/all_to_all | solution.py:86
  438.2 4.0 all-to-all-start.7
  443.0 6.1 %all-to-all-done.7 = f32[4,72,256]{2,1,0:T(8,128)S(1)} async-done(((f32[4,72,256]{2,1,0:T(8,128)}), f32[4,72,256]{2,1,0:T(8,128)S(1)}, u32[]{:S(2)}, u32[]{:S(2)}) %all-to-all-start.7) | async-done | bytes 294944 | tf_op jit(solution)/shard_map/all_to_all | solution.py:86
  (297 shorter events, 80.0 us)
Async XLA Ops:
  7.2 93.9 %copy-start.53 = (bf16[128,2048]{1,0:T(8,128)(2,1)S(1)}, bf16[128,2048]{1,0:T(8,128)(2,1)}, u32[]{:S(2)}) copy-start(bf16[128,2048]{1,0:T(8,128)(2,1)} %param.13) | copy-start | bytes 1572868
  7.2 143.9 %all-gather.7.cloned.1.call-start = ((), (), s32[]{:S(2)}) async-start(), calls=%async_computation.9 | async-start | bytes 4423680 | tf_op jit(solution)/shard_map/all_gather | solution.py:68
  63.4 20.6 %all-to-all-start = ((f32[8,1,16]{2,1,0:T(1,128)}), f32[8,1,16]{2,1,0:T(1,128)S(1)}, u32[]{:S(2)}, u32[]{:S(2)}) async-start(f32[8,1,16]{2,1,0:T(1,128)} %broadcast_in_dim.10), calls=%async_computation | async-start | bytes 8192 | tf_op jit(solution)/shard_map/all_to_all | solution.py:13
  74.6 20.5 %collective-permute-start.4 = (bf16[2,4,32,256]{3,2,1,0:T(8,128)(2,1)S(1)}, bf16[2,4,32,256]{3,2,1,0:T(8,128)(2,1)S(1)}, u32[]{:S(2)}, u32[]{:S(2)}) collective-permute-start(bf16[2,4,32,256]{3,2,1,0:T(8,128)(2,1)S(1)} %slice.629), channel_id=1, source_target_pairs={{4,0},{8,4},{12,8},{16,12},{20,16},{24,20},{28,24},{5,1},{9,5},{13... | collective-permute-start | bytes 393224 | tf_op jit(solution)/shard_map/ppermute | solution.py:34
  85.3 4.4 collective-permute-start
  90.7 18.9 %all-to-all-start.1 = ((bf16[4,4,8,16,128]{4,3,2,1,0:T(8,128)(2,1)}), bf16[4,4,8,16,128]{4,3,2,1,0:T(8,128)(2,1)S(1)}, u32[]{:S(2)}, u32[]{:S(2)}) async-start(bf16[4,4,8,16,128]{4,3,2,1,0:T(8,128)(2,1)} %broadcast_in_dim.11), calls=%async_computation.1 | async-start | bytes 1048576 | tf_op jit(solution)/shard_map/all_to_all | solution.py:13
  95.1 134.7 %all-gather.5.cloned.1.call-start = ((), (), s32[]{:S(2)}) async-start(), calls=%async_computation.8 | async-start | bytes 3981312 | tf_op jit(solution)/shard_map/all_gather | solution.py:186
  95.2 19.7 %collective-permute-start.6 = (bf16[6,1,32,256]{3,2,1,0:T(8,128)(2,1)S(1)}, bf16[6,1,32,256]{3,2,1,0:T(8,128)(2,1)S(1)}, u32[]{:S(2)}, u32[]{:S(2)}) collective-permute-start(bf16[6,1,32,256]{3,2,1,0:T(8,128)(2,1)S(1)} %get-tuple-element.98), channel_id=1, source_target_pairs={{1,0},{2,1},{3,2},{5,4},{6,5},{7,6},{9,8},{10,9},{11,10},{13,12},{... | collective-permute-start | bytes 294920 | tf_op jit(solution)/shard_map/ppermute | solution.py:58
  96.5 18.4 %collective-permute-start.5 = (bf16[6,1,32,256]{3,2,1,0:T(8,128)(2,1)S(1)}, bf16[6,1,32,256]{3,2,1,0:T(8,128)(2,1)S(1)}, u32[]{:S(2)}, u32[]{:S(2)}) collective-permute-start(bf16[6,1,32,256]{3,2,1,0:T(8,128)(2,1)S(1)} %get-tuple-element.97), channel_id=1, source_target_pairs={{0,1},{1,2},{2,3},{4,5},{5,6},{6,7},{8,9},{9,10},{10,11},{12,13},{... | collective-permute-start | bytes 294920 | tf_op jit(solution)/shard_map/ppermute | solution.py:56
  111.3 33.2 %all-to-all-start.3 = ((bf16[4,128,2048]{1,2,0:T(8,128)(2,1)}), bf16[4,128,2048]{1,2,0:T(8,128)(2,1)S(1)}, u32[]{:S(2)}, u32[]{:S(2)}) async-start(bf16[4,128,2048]{1,2,0:T(8,128)(2,1)} %broadcast_in_dim.12), calls=%async_computation.3 | async-start | bytes 4194304 | tf_op jit(solution)/shard_map/all_to_all | solution.py:13
  153.5 133.6 %copy-start = (bf16[8,4,216,256]{3,2,1,0:T(8,128)(2,1)}, bf16[8,4,216,256]{3,2,1,0:T(8,128)(2,1)S(1)}, u32[]{:S(2)}) copy-start(bf16[8,4,216,256]{3,2,1,0:T(8,128)(2,1)S(1)} %copy.79) | copy-start | bytes 10616836
  229.9 10.2 %copy-start.51 = (bf16[2,8,16,512]{3,2,1,0:T(8,128)(2,1)S(1)}, bf16[2,8,16,512]{3,2,1,0:T(8,128)(2,1)}, u32[]{:S(2)}) copy-start(bf16[2,8,16,512]{3,2,1,0:T(8,128)(2,1)} %get-tuple-element.60) | copy-start | bytes 786436
  229.9 10.4 %copy-start.50 = (bf16[2,8,16,512]{3,2,1,0:T(8,128)(2,1)S(1)}, bf16[2,8,16,512]{3,2,1,0:T(8,128)(2,1)}, u32[]{:S(2)}) copy-start(bf16[2,8,16,512]{3,2,1,0:T(8,128)(2,1)} %get-tuple-element.61) | copy-start | bytes 786436
  229.9 10.7 %copy-start.49 = (bf16[2,8,16,512]{3,2,1,0:T(8,128)(2,1)S(1)}, bf16[2,8,16,512]{3,2,1,0:T(8,128)(2,1)}, u32[]{:S(2)}) copy-start(bf16[2,8,16,512]{3,2,1,0:T(8,128)(2,1)} %get-tuple-element.62) | copy-start | bytes 786436
  229.9 10.9 %copy-start.48 = (bf16[2,8,16,512]{3,2,1,0:T(8,128)(2,1)S(1)}, bf16[2,8,16,512]{3,2,1,0:T(8,128)(2,1)}, u32[]{:S(2)}) copy-start(bf16[2,8,16,512]{3,2,1,0:T(8,128)(2,1)} %get-tuple-element.63) | copy-start | bytes 786436
  231.2 9.8 %copy-start.47 = (bf16[2,8,16,512]{3,2,1,0:T(8,128)(2,1)S(1)}, bf16[2,8,16,512]{3,2,1,0:T(8,128)(2,1)}, u32[]{:S(2)}) copy-start(bf16[2,8,16,512]{3,2,1,0:T(8,128)(2,1)} %get-tuple-element.64) | copy-start | bytes 786436
  232.6 8.7 %copy-start.22 = (bf16[2,8,16,4,128]{4,3,2,1,0:T(4,128)(2,1)S(1)}, bf16[2,8,16,4,128]{4,3,2,1,0:T(4,128)(2,1)}, u32[]{:S(2)}) copy-start(bf16[2,8,16,4,128]{4,3,2,1,0:T(4,128)(2,1)} %copy.70) | copy-start | bytes 786436
  245.2 10.0 %all-to-all-start.2 = ((bf16[2,8,16,128]{3,2,0,1:T(8,128)(2,1)}), bf16[2,8,16,128]{3,2,0,1:T(8,128)(2,1)}, u32[]{:S(2)}, u32[]{:S(2)}) async-start(bf16[2,8,16,128]{3,2,0,1:T(8,128)(2,1)} %fusion.45), calls=%async_computation.2 | async-start | bytes 131072 | tf_op jit(solution)/shard_map/all_to_all | solution.py:191
  266.1 17.1 %all-to-all-start.4 = ((f32[32,1,64]{2,1,0:T(1,128)}), f32[32,1,64]{2,1,0:T(1,128)S(1)}, u32[]{:S(2)}, u32[]{:S(2)}) async-start(f32[32,1,64]{2,1,0:T(1,128)} %broadcast_in_dim.13), calls=%async_computation.4 | async-start | bytes 32768 | tf_op jit(solution)/shard_map/all_to_all | solution.py:13
  287.1 22.9 %copy-start.57 = (f32[256]{0:T(256)S(1)}, f32[256]{0:T(256)}, u32[]{:S(2)}) copy-start(f32[256]{0:T(256)} %param.14) | copy-start | bytes 3076
  287.1 24.3 %copy-start.58 = (f32[256]{0:T(256)S(1)}, f32[256]{0:T(256)}, u32[]{:S(2)}) copy-start(f32[256]{0:T(256)} %mul.160) | copy-start | bytes 3076
  287.1 24.3 %copy-start.59 = (f32[256]{0:T(256)S(1)}, f32[256]{0:T(256)}, u32[]{:S(2)}) copy-start(f32[256]{0:T(256)} %sub.74) | copy-start | bytes 3076
  287.1 24.3 %copy-start.60 = (f32[256]{0:T(256)S(1)}, f32[256]{0:T(256)}, u32[]{:S(2)}) copy-start(f32[256]{0:T(256)} %param.15) | copy-start | bytes 3076
  289.9 37.0 %copy-start.8 = (bf16[4,4,32,256]{3,2,1,0:T(8,128)(2,1)S(1)}, bf16[4,4,32,256]{3,2,1,0:T(8,128)(2,1)}, u32[]{:S(2)}) copy-start(bf16[4,4,32,256]{3,2,1,0:T(8,128)(2,1)} %param.17) | copy-start | bytes 786436
  290.6 19.4 %all-to-all-start.5 = ((f32[32,1,512]{2,1,0:T(1,128)}), f32[32,1,512]{2,1,0:T(1,128)S(1)}, u32[]{:S(2)}, u32[]{:S(2)}) async-start(f32[32,1,512]{2,1,0:T(1,128)} %broadcast_in_dim.14), calls=%async_computation.5 | async-start | bytes 131072 | tf_op jit(solution)/shard_map/all_to_all | solution.py:13
  298.5 26.5 %copy-start.4 = (f32[4,4,32,256]{3,2,1,0:T(8,128)}, f32[4,4,32,256]{3,2,1,0:T(8,128)S(1)}, u32[]{:S(2)}) copy-start(f32[4,4,32,256]{3,2,1,0:T(8,128)S(1)} %reshape.484) | copy-start | bytes 1572868
  313.6 4.8 %collective-permute-start.1 = (bf16[2,4,32,256]{3,2,1,0:T(8,128)(2,1)S(1)}, bf16[2,4,32,256]{3,2,1,0:T(8,128)(2,1)S(1)}, u32[]{:S(2)}, u32[]{:S(2)}) collective-permute-start(bf16[2,4,32,256]{3,2,1,0:T(8,128)(2,1)S(1)} %slice.690), channel_id=1, source_target_pairs={{0,4},{4,8},{8,12},{12,16},{16,20},{20,24},{24,28},{1,5},{5,9},{9,... | collective-permute-start | bytes 393224 | tf_op jit(solution)/shard_map/ppermute | solution.py:34
  318.5 6.5 %collective-permute-start.3 = (bf16[6,1,32,256]{3,2,1,0:T(8,128)(2,1)S(1)}, bf16[6,1,32,256]{3,2,1,0:T(8,128)(2,1)S(1)}, u32[]{:S(2)}, u32[]{:S(2)}) collective-permute-start(bf16[6,1,32,256]{3,2,1,0:T(8,128)(2,1)S(1)} %get-tuple-element.104), channel_id=1, source_target_pairs={{1,0},{2,1},{3,2},{5,4},{6,5},{7,6},{9,8},{10,9},{11,10},{13,12},{... | collective-permute-start | bytes 294920 | tf_op jit(solution)/shard_map/ppermute | solution.py:58
  319.8 6.8 %collective-permute-start.2 = (bf16[6,1,32,256]{3,2,1,0:T(8,128)(2,1)S(1)}, bf16[6,1,32,256]{3,2,1,0:T(8,128)(2,1)S(1)}, u32[]{:S(2)}, u32[]{:S(2)}) collective-permute-start(bf16[6,1,32,256]{3,2,1,0:T(8,128)(2,1)S(1)} %get-tuple-element.103), channel_id=1, source_target_pairs={{0,1},{1,2},{2,3},{4,5},{5,6},{6,7},{8,9},{9,10},{10,11},{12,13},{... | collective-permute-start | bytes 294920 | tf_op jit(solution)/shard_map/ppermute | solution.py:56
  330.8 106.5 %all-to-all-start.6 = ((f32[8,288,256]{2,1,0:T(8,128)}), f32[8,288,256]{2,1,0:T(8,128)S(1)}, u32[]{:S(2)}, u32[]{:S(2)}) async-start(f32[8,288,256]{2,1,0:T(8,128)} %bitcast.329), calls=%async_computation.6 | async-start | bytes 4718592 | tf_op jit(solution)/shard_map/all_to_all | solution.py:86
  345.0 97.2 %copy-start.5 = (f32[4,4,32,256]{3,2,1,0:T(8,128)S(1)}, f32[4,4,32,256]{3,2,1,0:T(8,128)}, u32[]{:S(2)}) copy-start(f32[4,4,32,256]{3,2,1,0:T(8,128)} %copy-done.4) | copy-start | bytes 1572868
  438.2 10.8 %all-to-all-start.7 = ((f32[4,72,256]{2,1,0:T(8,128)}), f32[4,72,256]{2,1,0:T(8,128)S(1)}, u32[]{:S(2)}, u32[]{:S(2)}) async-start(f32[4,72,256]{2,1,0:T(8,128)} %bitcast.332), calls=%async_computation.7 | async-start | bytes 589824 | tf_op jit(solution)/shard_map/all_to_all | solution.py:86
  (46 other events, 112.8 us)
Sparse Core Ops, SparseCore 0:
  61.5 69.8 all-gather.6
  133.5 96.3 all-gather.4
where the time goes:
time: 458 us; the launch traced here: 457 us
  waiting for transfers between devices  228 us (50%)
  starting transfers between devices  60.9 us (13%)
  blocking collectives  54.2 us (12%)
  local copies, waits for them, and re-layouts  41.6 us (9%)
  matrix products  40.5 us (9%)
  between operations  15.6 us (3%)
  other arithmetic  15.3 us (3%)
    all_to_all x2, waiting for transfers between devices, sum_at_owner(): lax.all_to_all(tiles, axis, split_axis=0, concat_axis=0, tiled=True)  97.7 us
    all_gather x1, waiting for transfers between devices, local(): latent_weight = lax.all_gather(conv_latent, 'tm', axis=0, tiled=True)  68.7 us
    all_gather x1, blocking collectives, gather_in_order(): tiles = lax.all_gather(tiles, axes[k])  54.2 us
    all_to_all x5, waiting for transfers between devices, copy_for_each(): lax.all_to_all(jnp.broadcast_to(array[None], (devices, *array.shape)), ax...  52.8 us
    all_to_all x5, starting transfers between devices, copy_for_each(): lax.all_to_all(jnp.broadcast_to(array[None], (devices, *array.shape)), ax...  29.7 us
    dot_general x54, matrix products, causal_taps(): jnp.dot(window.reshape(-1, channels_in), kernel, preferred_element_type=j...  20.3 us
    dot_general x27, matrix products, transposed_taps(): lax.dot_general(window.reshape(-1, channels_out), kernel, (((1,), (1,)),...  14 us
    all_to_all x2, starting transfers between devices, sum_at_owner(): lax.all_to_all(tiles, axis, split_axis=0, concat_axis=0, tiled=True)  9.22 us
  transfers between devices with their start and end apart: 17, of which 13 were waited for; matrix products, arithmetic and copies ran while one was open for 12% of the time, Pallas kernels for 0%

commit v1 on v0

--- a/solution.py
+++ b/solution.py
@@ -188,7 +188,12 @@
     mixed = causal_taps(padded, latent_weight, frames_latent, rows_latent, cols_latent)
     refined = (latent_f32 + mixed).astype(jnp.bfloat16)
     band_rows = rows_latent // lax.axis_size("height")
-    own_band = lax.all_to_all(refined, "height", split_axis=1, concat_axis=3, tiled=True)
+    own_band = jnp.concatenate(
+        lax.all_to_all(
+            jnp.stack(jnp.split(refined, lax.axis_size("height"), axis=1)), "height", 0, 0
+        ),
+        axis=3,
+    )
     flat_band = own_band.reshape(-1, own_band.shape[-1])
     expanded = jnp.dot(
         flat_band, gather_directly(up_weight, "height", 0), preferred_element_type=jnp.float32

time: 458 us -> 458 us (level)
  no operation moved by 1% of the time
where the time goes in v1:
time: 458 us; the launch traced here: 457 us
  waiting for transfers between devices  228 us (50%)
  starting transfers between devices  61 us (13%)
  blocking collectives  54.2 us (12%)
  local copies, waits for them, and re-layouts  41.6 us (9%)
  matrix products  40.6 us (9%)
  between operations  15.6 us (3%)
  other arithmetic  15.3 us (3%)
    all_to_all x2, waiting for transfers between devices, sum_at_owner(): lax.all_to_all(tiles, axis, split_axis=0, concat_axis=0, tiled=True)  97.6 us
    all_gather x1, waiting for transfers between devices, local(): latent_weight = lax.all_gather(conv_latent, 'tm', axis=0, tiled=True)  68.7 us
    all_gather x1, blocking collectives, gather_in_order(): tiles = lax.all_gather(tiles, axes[k])  54.2 us
    all_to_all x5, waiting for transfers between devices, copy_for_each(): lax.all_to_all(jnp.broadcast_to(array[None], (devices, *array.shape)), ax...  52.8 us
    all_to_all x5, starting transfers between devices, copy_for_each(): lax.all_to_all(jnp.broadcast_to(array[None], (devices, *array.shape)), ax...  29.7 us
    dot_general x54, matrix products, causal_taps(): jnp.dot(window.reshape(-1, channels_in), kernel, preferred_element_type=j...  20.4 us
    dot_general x27, matrix products, transposed_taps(): lax.dot_general(window.reshape(-1, channels_out), kernel, (((1,), (1,)),...  14 us
    all_to_all x2, starting transfers between devices, sum_at_owner(): lax.all_to_all(tiles, axis, split_axis=0, concat_axis=0, tiled=True)  9.23 us
  transfers between devices with their start and end apart: 17, of which 13 were waited for; matrix products, arithmetic and copies ran while one was open for 12% of the time, Pallas kernels for 0%

profile of v1, /device:TPU:2, one launch (start us, length us, event | category | flops | bytes accessed | tf_op | source)
XLA Modules:
  0.0 456.6 jit_solution(9781808321123487798)
XLA Ops:
  7.2 54.2 %all-gather = bf16[1728,256]{1,0:T(8,128)(2,1)} all-gather(bf16[216,256]{1,0:T(8,128)(2,1)} %param.16), channel_id=2, replica_groups=mesh['dp'=16,'tm'=8,'height'=4] {'tm'}, dimensions={0}, use_global_device_ids=true | all-gather | bytes 995328 | tf_op jit(solution)/shard_map/all_gather | solution.py:68
  63.4 10.3 %all-to-all-start = ((f32[8,1,16]{2,1,0:T(1,128)}), f32[8,1,16]{2,1,0:T(1,128)S(1)}, u32[]{:S(2)}, u32[]{:S(2)}) async-start(f32[8,1,16]{2,1,0:T(1,128)} %broadcast_in_dim.10), calls=%async_computation | async-start | bytes 8192 | tf_op jit(solution)/shard_map/all_to_all | solution.py:13
  75.9 8.1 %all-to-all-done = f32[8,1,16]{2,1,0:T(1,128)S(1)} async-done(((f32[8,1,16]{2,1,0:T(1,128)}), f32[8,1,16]{2,1,0:T(1,128)S(1)}, u32[]{:S(2)}, u32[]{:S(2)}) %all-to-all-start) | async-done | bytes 544 | tf_op jit(solution)/shard_map/all_to_all | solution.py:13
  85.3 2.5 collective-permute-start
  90.7 4.5 all-to-all-start.1
  96.5 4.6 collective-permute-start.5
  101.3 8.3 %all-to-all-done.1 = bf16[4,4,8,16,128]{4,3,2,1,0:T(8,128)(2,1)S(1)} async-done(((bf16[4,4,8,16,128]{4,3,2,1,0:T(8,128)(2,1)}), bf16[4,4,8,16,128]{4,3,2,1,0:T(8,128)(2,1)S(1)}, u32[]{:S(2)}, u32[]{:S(2)}) %all-to-all-start.1) | async-done | bytes 524320 | tf_op jit(solution)/shard_map/all_to_all | solution.py:13
  111.3 3.6 all-to-all-start.3
  123.0 2.4 pad_slice_fusion
  125.4 19.1 %all-to-all-done.3 = bf16[4,128,2048]{1,2,0:T(8,128)(2,1)S(1)} async-done(((bf16[4,128,2048]{1,2,0:T(8,128)(2,1)}), bf16[4,128,2048]{1,2,0:T(8,128)(2,1)S(1)}, u32[]{:S(2)}, u32[]{:S(2)}) %all-to-all-start.3) | async-done | bytes 2097184 | tf_op jit(solution)/shard_map/all_to_all | solution.py:13
  144.5 2.6 copy.63
  147.2 3.9 copy.64
  151.1 2.4 copy.67
  161.2 68.7 %all-gather.5.cloned.1.call-done = bf16[13824,128]{1,0:T(8,128)(2,1)} async-done(((bf16[1728,128]{1,0:T(8,128)(2,1)}), bf16[13824,128]{1,0:T(8,128)(2,1)}) %all-gather.5.cloned.1.call-update) | async-done | bytes 3538960 | tf_op jit(solution)/shard_map/all_gather | solution.py:186
  245.2 4.3 all-to-all-start.2
  251.6 3.6 all-to-all-done.2
  258.2 3.8 fusion.146
  266.1 4.8 %all-to-all-start.4 = ((f32[32,1,64]{2,1,0:T(1,128)}), f32[32,1,64]{2,1,0:T(1,128)S(1)}, u32[]{:S(2)}, u32[]{:S(2)}) async-start(f32[32,1,64]{2,1,0:T(1,128)} %broadcast_in_dim.13), calls=%async_computation.4 | async-start | bytes 32768 | tf_op jit(solution)/shard_map/all_to_all | solution.py:13
  273.0 2.2 copy.65
  275.2 2.2 reshape.487
  277.4 5.9 %all-to-all-done.4 = f32[32,1,64]{2,1,0:T(1,128)S(1)} async-done(((f32[32,1,64]{2,1,0:T(1,128)}), f32[32,1,64]{2,1,0:T(1,128)S(1)}, u32[]{:S(2)}, u32[]{:S(2)}) %all-to-all-start.4) | async-done | bytes 8224 | tf_op jit(solution)/shard_map/all_to_all | solution.py:13
  287.2 2.8 fusion.145
  290.6 6.5 %all-to-all-start.5 = ((f32[32,1,512]{2,1,0:T(1,128)}), f32[32,1,512]{2,1,0:T(1,128)S(1)}, u32[]{:S(2)}, u32[]{:S(2)}) async-start(f32[32,1,512]{2,1,0:T(1,128)} %broadcast_in_dim.14), calls=%async_computation.5 | async-start | bytes 131072 | tf_op jit(solution)/shard_map/all_to_all | solution.py:13
  298.6 11.5 %all-to-all-done.5 = f32[32,1,512]{2,1,0:T(1,128)S(1)} async-done(((f32[32,1,512]{2,1,0:T(1,128)}), f32[32,1,512]{2,1,0:T(1,128)S(1)}, u32[]{:S(2)}, u32[]{:S(2)}) %all-to-all-start.5) | async-done | bytes 65568 | tf_op jit(solution)/shard_map/all_to_all | solution.py:13
  311.5 2.2 add_convert_fusion
  313.7 2.3 collective-permute-start.1
  316.0 2.5 collective-permute-done.1
  319.8 4.6 collective-permute-start.2
  330.9 5.2 %all-to-all-start.6 = ((f32[8,288,256]{2,1,0:T(8,128)}), f32[8,288,256]{2,1,0:T(8,128)S(1)}, u32[]{:S(2)}, u32[]{:S(2)}) async-start(f32[8,288,256]{2,1,0:T(8,128)} %bitcast.334), calls=%async_computation.6 | async-start | bytes 4718592 | tf_op jit(solution)/shard_map/all_to_all | solution.py:86
  345.8 91.5 %all-to-all-done.6 = f32[8,288,256]{2,1,0:T(8,128)S(1)} async-done(((f32[8,288,256]{2,1,0:T(8,128)}), f32[8,288,256]{2,1,0:T(8,128)S(1)}, u32[]{:S(2)}, u32[]{:S(2)}) %all-to-all-start.6) | async-done | bytes 2359328 | tf_op jit(solution)/shard_map/all_to_all | solution.py:86
  438.2 4.0 all-to-all-start.7
  443.0 6.1 %all-to-all-done.7 = f32[4,72,256]{2,1,0:T(8,128)S(1)} async-done(((f32[4,72,256]{2,1,0:T(8,128)}), f32[4,72,256]{2,1,0:T(8,128)S(1)}, u32[]{:S(2)}, u32[]{:S(2)}) %all-to-all-start.7) | async-done | bytes 294944 | tf_op jit(solution)/shard_map/all_to_all | solution.py:86
  (294 shorter events, 80.0 us)
Async XLA Ops:
  7.2 93.9 %copy-start.51 = (bf16[128,2048]{1,0:T(8,128)(2,1)S(1)}, bf16[128,2048]{1,0:T(8,128)(2,1)}, u32[]{:S(2)}) copy-start(bf16[128,2048]{1,0:T(8,128)(2,1)} %param.13) | copy-start | bytes 1572868
  7.2 143.9 %all-gather.7.cloned.1.call-start = ((), (), s32[]{:S(2)}) async-start(), calls=%async_computation.9 | async-start | bytes 4423680 | tf_op jit(solution)/shard_map/all_gather | solution.py:68
  63.4 20.6 %all-to-all-start = ((f32[8,1,16]{2,1,0:T(1,128)}), f32[8,1,16]{2,1,0:T(1,128)S(1)}, u32[]{:S(2)}, u32[]{:S(2)}) async-start(f32[8,1,16]{2,1,0:T(1,128)} %broadcast_in_dim.10), calls=%async_computation | async-start | bytes 8192 | tf_op jit(solution)/shard_map/all_to_all | solution.py:13
  74.6 20.5 %collective-permute-start.4 = (bf16[2,4,32,256]{3,2,1,0:T(8,128)(2,1)S(1)}, bf16[2,4,32,256]{3,2,1,0:T(8,128)(2,1)S(1)}, u32[]{:S(2)}, u32[]{:S(2)}) collective-permute-start(bf16[2,4,32,256]{3,2,1,0:T(8,128)(2,1)S(1)} %slice.629), channel_id=1, source_target_pairs={{4,0},{8,4},{12,8},{16,12},{20,16},{24,20},{28,24},{5,1},{9,5},{13... | collective-permute-start | bytes 393224 | tf_op jit(solution)/shard_map/ppermute | solution.py:34
  85.3 4.4 collective-permute-start
  90.7 19.0 %all-to-all-start.1 = ((bf16[4,4,8,16,128]{4,3,2,1,0:T(8,128)(2,1)}), bf16[4,4,8,16,128]{4,3,2,1,0:T(8,128)(2,1)S(1)}, u32[]{:S(2)}, u32[]{:S(2)}) async-start(bf16[4,4,8,16,128]{4,3,2,1,0:T(8,128)(2,1)} %broadcast_in_dim.11), calls=%async_computation.1 | async-start | bytes 1048576 | tf_op jit(solution)/shard_map/all_to_all | solution.py:13
  95.1 134.7 %all-gather.5.cloned.1.call-start = ((), (), s32[]{:S(2)}) async-start(), calls=%async_computation.8 | async-start | bytes 3981312 | tf_op jit(solution)/shard_map/all_gather | solution.py:186
  95.2 19.7 %collective-permute-start.6 = (bf16[6,1,32,256]{3,2,1,0:T(8,128)(2,1)S(1)}, bf16[6,1,32,256]{3,2,1,0:T(8,128)(2,1)S(1)}, u32[]{:S(2)}, u32[]{:S(2)}) collective-permute-start(bf16[6,1,32,256]{3,2,1,0:T(8,128)(2,1)S(1)} %get-tuple-element.98), channel_id=1, source_target_pairs={{1,0},{2,1},{3,2},{5,4},{6,5},{7,6},{9,8},{10,9},{11,10},{13,12},{... | collective-permute-start | bytes 294920 | tf_op jit(solution)/shard_map/ppermute | solution.py:58
  96.5 18.4 %collective-permute-start.5 = (bf16[6,1,32,256]{3,2,1,0:T(8,128)(2,1)S(1)}, bf16[6,1,32,256]{3,2,1,0:T(8,128)(2,1)S(1)}, u32[]{:S(2)}, u32[]{:S(2)}) collective-permute-start(bf16[6,1,32,256]{3,2,1,0:T(8,128)(2,1)S(1)} %get-tuple-element.97), channel_id=1, source_target_pairs={{0,1},{1,2},{2,3},{4,5},{5,6},{6,7},{8,9},{9,10},{10,11},{12,13},{... | collective-permute-start | bytes 294920 | tf_op jit(solution)/shard_map/ppermute | solution.py:56
  111.3 33.2 %all-to-all-start.3 = ((bf16[4,128,2048]{1,2,0:T(8,128)(2,1)}), bf16[4,128,2048]{1,2,0:T(8,128)(2,1)S(1)}, u32[]{:S(2)}, u32[]{:S(2)}) async-start(bf16[4,128,2048]{1,2,0:T(8,128)(2,1)} %broadcast_in_dim.12), calls=%async_computation.3 | async-start | bytes 4194304 | tf_op jit(solution)/shard_map/all_to_all | solution.py:13
  153.5 133.7 %copy-start = (bf16[8,4,216,256]{3,2,1,0:T(8,128)(2,1)}, bf16[8,4,216,256]{3,2,1,0:T(8,128)(2,1)S(1)}, u32[]{:S(2)}) copy-start(bf16[8,4,216,256]{3,2,1,0:T(8,128)(2,1)S(1)} %copy.67) | copy-start | bytes 10616836
  229.9 10.2 %copy-start.49 = (bf16[2,8,16,512]{3,2,1,0:T(8,128)(2,1)S(1)}, bf16[2,8,16,512]{3,2,1,0:T(8,128)(2,1)}, u32[]{:S(2)}) copy-start(bf16[2,8,16,512]{3,2,1,0:T(8,128)(2,1)} %get-tuple-element.60) | copy-start | bytes 786436
  229.9 10.4 %copy-start.48 = (bf16[2,8,16,512]{3,2,1,0:T(8,128)(2,1)S(1)}, bf16[2,8,16,512]{3,2,1,0:T(8,128)(2,1)}, u32[]{:S(2)}) copy-start(bf16[2,8,16,512]{3,2,1,0:T(8,128)(2,1)} %get-tuple-element.61) | copy-start | bytes 786436
  229.9 10.7 %copy-start.47 = (bf16[2,8,16,512]{3,2,1,0:T(8,128)(2,1)S(1)}, bf16[2,8,16,512]{3,2,1,0:T(8,128)(2,1)}, u32[]{:S(2)}) copy-start(bf16[2,8,16,512]{3,2,1,0:T(8,128)(2,1)} %get-tuple-element.62) | copy-start | bytes 786436
  229.9 10.9 %copy-start.46 = (bf16[2,8,16,512]{3,2,1,0:T(8,128)(2,1)S(1)}, bf16[2,8,16,512]{3,2,1,0:T(8,128)(2,1)}, u32[]{:S(2)}) copy-start(bf16[2,8,16,512]{3,2,1,0:T(8,128)(2,1)} %get-tuple-element.63) | copy-start | bytes 786436
  231.2 9.8 %copy-start.45 = (bf16[2,8,16,512]{3,2,1,0:T(8,128)(2,1)S(1)}, bf16[2,8,16,512]{3,2,1,0:T(8,128)(2,1)}, u32[]{:S(2)}) copy-start(bf16[2,8,16,512]{3,2,1,0:T(8,128)(2,1)} %get-tuple-element.64) | copy-start | bytes 786436
  232.6 8.7 %copy-start.20 = (bf16[2,8,16,4,128]{4,3,2,1,0:T(4,128)(2,1)S(1)}, bf16[2,8,16,4,128]{4,3,2,1,0:T(4,128)(2,1)}, u32[]{:S(2)}) copy-start(bf16[2,8,16,4,128]{4,3,2,1,0:T(4,128)(2,1)} %copy.59) | copy-start | bytes 786436
  245.2 10.0 %all-to-all-start.2 = ((bf16[4,2,2,16,128]{4,3,2,1,0:T(8,128)(2,1)}), bf16[4,2,2,16,128]{4,3,2,1,0:T(8,128)(2,1)}, u32[]{:S(2)}, u32[]{:S(2)}) async-start(bf16[4,2,2,16,128]{4,3,2,1,0:T(8,128)(2,1)} %pad_maximum_fusion.5), calls=%async_computation.2 | async-start | bytes 131072 | tf_op jit(solution)/shard_map/all_to_all | solution.py:192
  266.1 17.2 %all-to-all-start.4 = ((f32[32,1,64]{2,1,0:T(1,128)}), f32[32,1,64]{2,1,0:T(1,128)S(1)}, u32[]{:S(2)}, u32[]{:S(2)}) async-start(f32[32,1,64]{2,1,0:T(1,128)} %broadcast_in_dim.13), calls=%async_computation.4 | async-start | bytes 32768 | tf_op jit(solution)/shard_map/all_to_all | solution.py:13
  287.2 22.9 %copy-start.55 = (f32[256]{0:T(256)S(1)}, f32[256]{0:T(256)}, u32[]{:S(2)}) copy-start(f32[256]{0:T(256)} %param.14) | copy-start | bytes 3076
  287.2 24.2 %copy-start.56 = (f32[256]{0:T(256)S(1)}, f32[256]{0:T(256)}, u32[]{:S(2)}) copy-start(f32[256]{0:T(256)} %mul.160) | copy-start | bytes 3076
  287.2 24.3 %copy-start.57 = (f32[256]{0:T(256)S(1)}, f32[256]{0:T(256)}, u32[]{:S(2)}) copy-start(f32[256]{0:T(256)} %sub.74) | copy-start | bytes 3076
  287.2 24.3 %copy-start.58 = (f32[256]{0:T(256)S(1)}, f32[256]{0:T(256)}, u32[]{:S(2)}) copy-start(f32[256]{0:T(256)} %param.15) | copy-start | bytes 3076
  290.0 37.0 %copy-start.6 = (bf16[4,4,32,256]{3,2,1,0:T(8,128)(2,1)S(1)}, bf16[4,4,32,256]{3,2,1,0:T(8,128)(2,1)}, u32[]{:S(2)}) copy-start(bf16[4,4,32,256]{3,2,1,0:T(8,128)(2,1)} %param.17) | copy-start | bytes 786436
  290.6 19.4 %all-to-all-start.5 = ((f32[32,1,512]{2,1,0:T(1,128)}), f32[32,1,512]{2,1,0:T(1,128)S(1)}, u32[]{:S(2)}, u32[]{:S(2)}) async-start(f32[32,1,512]{2,1,0:T(1,128)} %broadcast_in_dim.14), calls=%async_computation.5 | async-start | bytes 131072 | tf_op jit(solution)/shard_map/all_to_all | solution.py:13
  298.6 28.9 %copy-start.2 = (f32[4,4,32,256]{3,2,1,0:T(8,128)}, f32[4,4,32,256]{3,2,1,0:T(8,128)S(1)}, u32[]{:S(2)}) copy-start(f32[4,4,32,256]{3,2,1,0:T(8,128)S(1)} %reshape.486) | copy-start | bytes 1572868
  313.7 4.8 %collective-permute-start.1 = (bf16[2,4,32,256]{3,2,1,0:T(8,128)(2,1)S(1)}, bf16[2,4,32,256]{3,2,1,0:T(8,128)(2,1)S(1)}, u32[]{:S(2)}, u32[]{:S(2)}) collective-permute-start(bf16[2,4,32,256]{3,2,1,0:T(8,128)(2,1)S(1)} %slice.690), channel_id=1, source_target_pairs={{0,4},{4,8},{8,12},{12,16},{16,20},{20,24},{24,28},{1,5},{5,9},{9,... | collective-permute-start | bytes 393224 | tf_op jit(solution)/shard_map/ppermute | solution.py:34
  318.5 6.5 %collective-permute-start.3 = (bf16[6,1,32,256]{3,2,1,0:T(8,128)(2,1)S(1)}, bf16[6,1,32,256]{3,2,1,0:T(8,128)(2,1)S(1)}, u32[]{:S(2)}, u32[]{:S(2)}) collective-permute-start(bf16[6,1,32,256]{3,2,1,0:T(8,128)(2,1)S(1)} %get-tuple-element.104), channel_id=1, source_target_pairs={{1,0},{2,1},{3,2},{5,4},{6,5},{7,6},{9,8},{10,9},{11,10},{13,12},{... | collective-permute-start | bytes 294920 | tf_op jit(solution)/shard_map/ppermute | solution.py:58
  319.8 6.8 %collective-permute-start.2 = (bf16[6,1,32,256]{3,2,1,0:T(8,128)(2,1)S(1)}, bf16[6,1,32,256]{3,2,1,0:T(8,128)(2,1)S(1)}, u32[]{:S(2)}, u32[]{:S(2)}) collective-permute-start(bf16[6,1,32,256]{3,2,1,0:T(8,128)(2,1)S(1)} %get-tuple-element.103), channel_id=1, source_target_pairs={{0,1},{1,2},{2,3},{4,5},{5,6},{6,7},{8,9},{9,10},{10,11},{12,13},{... | collective-permute-start | bytes 294920 | tf_op jit(solution)/shard_map/ppermute | solution.py:56
  330.9 106.5 %all-to-all-start.6 = ((f32[8,288,256]{2,1,0:T(8,128)}), f32[8,288,256]{2,1,0:T(8,128)S(1)}, u32[]{:S(2)}, u32[]{:S(2)}) async-start(f32[8,288,256]{2,1,0:T(8,128)} %bitcast.334), calls=%async_computation.6 | async-start | bytes 4718592 | tf_op jit(solution)/shard_map/all_to_all | solution.py:86
  345.1 97.1 %copy-start.3 = (f32[4,4,32,256]{3,2,1,0:T(8,128)S(1)}, f32[4,4,32,256]{3,2,1,0:T(8,128)}, u32[]{:S(2)}) copy-start(f32[4,4,32,256]{3,2,1,0:T(8,128)} %copy-done.2) | copy-start | bytes 1572868
  438.2 10.8 %all-to-all-start.7 = ((f32[4,72,256]{2,1,0:T(8,128)}), f32[4,72,256]{2,1,0:T(8,128)S(1)}, u32[]{:S(2)}, u32[]{:S(2)}) async-start(f32[4,72,256]{2,1,0:T(8,128)} %bitcast.337), calls=%async_computation.7 | async-start | bytes 589824 | tf_op jit(solution)/shard_map/all_to_all | solution.py:86
  (44 other events, 109.1 us)
Sparse Core Ops, SparseCore 0:
  61.5 69.8 all-gather.6
  133.5 96.2 all-gather.4
